TPU v7x, 32 devices: a whole 2x2x4 slice. The times are simulated.
32 devices in a mesh: particle: 8 (over z, x), token: 4 (over y, core).
Axes of the slice: x: 2, y: 2, z: 4, core: 2. Of those that a mesh axis runs over, the one named last changes fastest.
Arguments:
- states: bfloat16 [16, 256, 768], P('particle', 'token'), may hold values from -6 to 6
- ancestors: int32 [16], P('particle'), may hold values from 0 to 15, as said below
- pair_bias: bfloat16 [16, 256, 256], P(None, 'token'), may hold values from -3 to 300, as said below
- key_mask: int32 [256], replicated, may hold values from 0 to 1, as said below
- gain_attn: float32 [768], replicated, may hold values from 0.1 to 1.9
- w_qkv: bfloat16 [768, 2304], replicated, may hold values from -0.21875 to 0.21875
- w_o: bfloat16 [768, 768], replicated, may hold values from -0.21875 to 0.21875
- gain_ff: float32 [768], replicated, may hold values from 0.1 to 1.9
- w_in: bfloat16 [2, 768, 1536], P(None, 'particle'), may hold values from -0.21875 to 0.21875
- w_out: bfloat16 [768, 1536], P('particle'), may hold values from -0.15625 to 0.15625
Outputs:
- new_states: bfloat16 [16, 256, 768], P('particle', 'token')
Inputs may be any that keep to these rules, and one draw needn't show every extreme that they name: `ancestors`: any particle may be the ancestor of any number of particles. `pair_bias`: real values; rows of some heads may hold a few large entries. `key_mask`: 1 on a prefix of 128 or more tokens and 0 after it; the last token is always 0.
All inputs are finite; a program needn't handle non-finite values.
Results may differ from a plain program's by a relative error of at most 0.0085.
Values may be sent and summed in bfloat16 or wider, within the bound.
A program may use at most 64 MiB of HBM per device.

v0:
```python
import math

import jax
import jax.numpy as jnp
from jax import lax
from jax.sharding import PartitionSpec as P


def rms_norm(stream, gain_vec):
    return stream * lax.rsqrt(jnp.mean(stream * stream, axis=-1, keepdims=True) + 1e-05) * gain_vec


def attend_portion(running_sum, queries, key_part, value_part, pair_bias, key_mask):
    running, totals, summed = running_sum
    part_count, row_count, model_width = queries.shape
    head_count = pair_bias.shape[0]
    head_size = model_width // head_count
    number = key_part.shape[1]
    query_heads = queries.reshape(part_count, row_count, head_count, head_size)
    key_heads = key_part.reshape(part_count, number, head_count, head_size)
    value_heads = value_part.reshape(part_count, number, head_count, head_size)
    scores = jnp.einsum(
        "prhe,pnhe->phrn", query_heads, key_heads, preferred_element_type=jnp.float32
    )
    bias_part = pair_bias.astype(jnp.float32)
    scores = scores + bias_part[None]
    usable = (key_mask > 0)[None, None, None, :]
    new_max = jnp.maximum(running, jnp.max(jnp.where(usable, scores, -1e30), axis=3))
    weights = jnp.where(usable, jnp.exp(scores - new_max[..., None]), 0.0)
    totals = jnp.sum(weights, axis=3)
    summed = jnp.einsum(
        "phrn,pnhe->phre",
        weights.astype(jnp.bfloat16),
        value_heads,
        preferred_element_type=jnp.float32,
    )
    return (new_max, totals, summed)


def run_block(states, pair_bias, key_mask, gain_attn, w_qkv, w_o, gain_ff, w_in, w_out):
    part_count, row_count, model_width = states.shape
    head_count = pair_bias.shape[0]
    head_size = model_width // head_count
    score_scale = 1.0 / math.sqrt(head_size)
    stream = states.astype(jnp.float32)
    normed = rms_norm(stream, gain_attn).astype(jnp.bfloat16)
    start_carry = (
        jnp.full((part_count, head_count, row_count), -1e30, jnp.float32),
        jnp.zeros((part_count, head_count, row_count), jnp.float32),
        jnp.zeros((part_count, head_count, row_count, head_size), jnp.float32),
    )
    projected = jnp.einsum("prd,de->pre", normed, w_qkv, preferred_element_type=jnp.float32)
    queries = (projected[..., :model_width] * score_scale).astype(jnp.bfloat16)
    key_local = projected[..., model_width : 2 * model_width].astype(jnp.bfloat16)
    value_local = projected[..., 2 * model_width :].astype(jnp.bfloat16)
    portion = (
        lax.all_gather(key_local, "token", axis=1, tiled=True),
        lax.all_gather(value_local, "token", axis=1, tiled=True),
    )
    running, totals, summed = attend_portion(
        start_carry, queries, portion[0], portion[1], pair_bias, key_mask
    )
    attended = (
        (summed / totals[..., None])
        .transpose(0, 2, 1, 3)
        .reshape(part_count, row_count, model_width)
        .astype(jnp.bfloat16)
    )
    stream = stream + jnp.einsum("prd,de->pre", attended, w_o, preferred_element_type=jnp.float32)
    normed_ff = rms_norm(stream, gain_ff).astype(jnp.bfloat16)
    portion = lax.all_gather(w_in, "particle", axis=1, tiled=True)
    gate_sum = jnp.einsum("prd,df->prf", normed_ff, portion[0], preferred_element_type=jnp.float32)
    up_sum = jnp.einsum("prd,df->prf", normed_ff, portion[1], preferred_element_type=jnp.float32)
    hidden = (jax.nn.silu(gate_sum) * up_sum).astype(jnp.bfloat16)
    update = jnp.einsum(
        "prf,nf->prn",
        hidden,
        lax.all_gather(w_out, "particle", axis=0, tiled=True),
        preferred_element_type=jnp.float32,
    )
    return (stream + update).astype(jnp.bfloat16)


def select_rows(ancestors, portion):
    number = portion.shape[0]
    indices = lax.iota(jnp.int32, number)
    onehot = (ancestors[:, None] == indices[None, :]).astype(jnp.bfloat16)
    return jnp.einsum("jp,prd->jrd", onehot, portion, preferred_element_type=jnp.float32)


def body(states, ancestors, pair_bias, key_mask, gain_attn, w_qkv, w_o, gain_ff, w_in, w_out):
    chosen = select_rows(ancestors, lax.all_gather(states, "particle", axis=0, tiled=True)).astype(
        jnp.bfloat16
    )
    return run_block(chosen, pair_bias, key_mask, gain_attn, w_qkv, w_o, gain_ff, w_in, w_out)


def solution(mesh):
    placed = (
        P("particle", "token", None),
        P("particle"),
        P(None, "token", None),
        P(),
        P(),
        P(),
        P(),
        P(),
        P(None, "particle", None),
        P("particle", None),
    )
    return jax.shard_map(
        body, mesh=mesh, in_specs=placed, out_specs=P("particle", "token", None), check_vma=False
    )
```

profile of v0, /device:TPU:0, one launch (start us, length us, event | category | flops | bytes accessed | tf_op | source)
XLA Modules:
  0.0 203.7 jit_solution(8194128986343021711)
XLA Ops:
  6.5 0.7 all-gather.4.cloned.1.call-update
  7.3 0.7 all-gather.6.cloned.1.call-update
  8.0 0.0 all-gather.8.cloned.1.call-start
  8.1 0.7 all-gather.8.cloned.1.call-update
  8.8 2.2 %convert_element_type.40 = f32[16,64,256]{2,1,0:T(8,128)} convert(bf16[16,64,256]{2,1,0:T(8,128)(2,1)} %param.12) | non-fusion elementwise | flops 262144 | bytes 1572864 | tf_op jit(solution)/shard_map/convert_element_type | solution.py:25
  11.0 45.5 %all-gather.4.cloned.1.call-done = bf16[16,64,768]{2,1,0:T(8,128)(2,1)} async-done(((bf16[2,64,768]{2,1,0:T(8,128)(2,1)}), bf16[16,64,768]{2,1,0:T(8,128)(2,1)}) %all-gather.4.cloned.1.call-update) | async-done | bytes 1572880 | tf_op jit(solution)/shard_map/all_gather | solution.py:92
  56.5 2.5 %multiply_reduce_fusion.1 = (f32[2,64]{0,1:T(8,128)S(1)}, f32[2,64,768]{2,0,1:T(2,128)S(1)}) fusion(bf16[16,64,768]{2,1,0:T(8,128)(2,1)} %all-gather.4.cloned.1.call-done, s32[2]{0:T(128)S(1)} %copy-done.10), kind=kOutput, calls=%fused_computation.40 | convolution fusion | flops 3538848 | bytes 1966600 | tf_op jit(solution)/shard_map/jp,prd->jrd/dot_general | solution.py:88
  59.0 0.7 copy-done.2
  59.7 0.2 multiply_convert_fusion.1
  60.0 1.7 fusion.44
  61.7 0.7 fusion.43
  62.4 9.0 %all_gather.16 = bf16[2,256,768]{2,1,0:T(8,128)(2,1)} all-gather(bf16[2,64,768]{2,1,0:T(8,128)(2,1)S(1)} %get-tuple-element.5), channel_id=1, replica_groups=mesh['particle'=8,'token'=4] {'token'}, dimensions={1}, use_global_device_ids=true | all-gather | bytes 983040 | tf_op jit(solution)/shard_map/all_gather | solution.py:57
  71.4 2.4 %copy.59 = bf16[2,256,768]{1,2,0:T(8,128)(2,1)} copy(bf16[2,256,768]{2,1,0:T(8,128)(2,1)} %all_gather.16) | data formatting | bytes 1572864 | tf_op jit(solution)/shard_map/all_gather | solution.py:57
  73.7 1.7 fusion.30
  75.5 1.9 copy.71
  77.3 9.8 %all_gather.17 = bf16[2,256,768]{2,1,0:T(8,128)(2,1)} all-gather(bf16[2,64,768]{2,1,0:T(8,128)(2,1)} %get-tuple-element.6), channel_id=1, replica_groups=mesh['particle'=8,'token'=4] {'token'}, dimensions={1}, use_global_device_ids=true | all-gather | bytes 983040 | tf_op jit(solution)/shard_map/all_gather | solution.py:58
  87.1 2.3 %copy.61 = bf16[2,256,768]{1,2,0:T(8,128)(2,1)} copy(bf16[2,256,768]{2,1,0:T(8,128)(2,1)} %all_gather.17) | data formatting | bytes 1572864 | tf_op jit(solution)/shard_map/all_gather | solution.py:58
  89.4 2.2 %select_reduce_fusion = (f32[2,16,64]{2,1,0:T(8,128)S(1)}, f32[2,16,64,256]{3,2,1,0:T(8,128)S(1)}) fusion(f32[16,64,256]{2,1,0:T(8,128)} %convert_element_type.40, pred[256]{0:T(512)(128)(4,1)S(1)} %broadcast_compare_fusion, bf16[2,64,16,48]{1,3,2,0:T(8,128)(2,1)} %bitcast.42, bf16[2,256,16,48]{1,3,2,0:T(8,128)(2,1)} %bitcast.41), kind=kOutput, calls=%fused_computation.10 | convolution fusion | flops 51902464 | bytes 4137216 | tf_op jit(solution)/shard_map/prhe,pnhe->phrn/dot_general | solution.py:22
  91.7 0.9 fusion.6
  92.6 0.2 copy-done.6
  92.8 0.6 fusion.11
  93.4 0.9 copy-done.5
  94.4 0.4 fusion.12
  94.7 0.4 multiply_reduce_fusion
  95.1 0.3 copy-done.4
  95.5 1.1 multiply_convert_fusion
  96.6 40.8 %all-gather.6.cloned.1.call-done = bf16[2,768,1536]{2,1,0:T(8,128)(2,1)} async-done(((bf16[2,96,1536]{2,1,0:T(8,128)(2,1)}), bf16[2,768,1536]{2,1,0:T(8,128)(2,1)}) %all-gather.6.cloned.1.call-update) | async-done | bytes 4718608 | tf_op jit(solution)/shard_map/all_gather | solution.py:71
  137.4 3.2 %fusion.3 = f32[2,64,1536]{2,1,0:T(8,128)} fusion(bf16[2,768,1536]{2,1,0:T(8,128)(2,1)} %all-gather.6.cloned.1.call-done, bf16[2,64,768]{2,0,1:T(2,128)(2,1)} %multiply_convert_fusion), kind=kOutput, calls=%fused_computation.6 | convolution fusion | flops 301989888 | bytes 3342336 | tf_op jit(solution)/shard_map/prd,df->prf/dot_general | solution.py:72
  140.6 49.2 %all-gather.8.cloned.1.call-done = bf16[768,1536]{1,0:T(8,128)(2,1)} async-done(((bf16[96,1536]{1,0:T(8,128)(2,1)}), bf16[768,1536]{1,0:T(8,128)(2,1)}) %all-gather.8.cloned.1.call-update) | async-done | bytes 2359312 | tf_op jit(solution)/shard_map/all_gather | solution.py:78
  189.8 4.8 %fusion.4 = f32[2,64,768]{2,1,0:T(8,128)} fusion(bf16[768,1536]{1,0:T(8,128)(2,1)} %all-gather.8.cloned.1.call-done, bf16[2,768,1536]{2,1,0:T(8,128)(2,1)} %all-gather.6.cloned.1.call-done, f32[2,64,1536]{2,1,0:T(8,128)} %fusion.3, bf16[2,64,768]{2,0,1:T(2,128)(2,1)} %multiply_convert_fusion), kind=kOutput, calls=%fused_computation.7 | convolution fusion | flops 605159424 | bytes 6094848 | tf_op jit(solution)/shard_map/prf,nf->prn/dot_general | solution.py:75
  194.6 1.8 fusion.31
  196.4 0.7 copy.69
  (24 shorter events, 0.1 us)
Async XLA Ops:
  6.5 53.4 %copy-start = (bf16[768,2304]{1,0:T(8,128)(2,1)S(1)}, bf16[768,2304]{1,0:T(8,128)(2,1)}, u32[]{:S(2)}) copy-start(bf16[768,2304]{1,0:T(8,128)(2,1)} %param.15) | copy-start | bytes 10616836
  6.5 4.4 %copy-start.9 = (s32[256]{0:T(256)S(1)}, s32[256]{0:T(256)}, u32[]{:S(2)}) copy-start(s32[256]{0:T(256)} %param.13) | copy-start | bytes 3076
  6.5 49.9 %copy-start.10 = (s32[2]{0:T(128)S(1)}, s32[2]{0:T(128)}, u32[]{:S(2)}) copy-start(s32[2]{0:T(128)} %param.11) | copy-start | bytes 28
  6.5 49.9 %all-gather.4.cloned.1.call-start = ((), (), s32[]{:S(2)}) async-start(), calls=%async_computation | async-start | bytes 1769472 | tf_op jit(solution)/shard_map/all_gather | solution.py:92
  7.3 130.1 %all-gather.6.cloned.1.call-start = ((), (), s32[]{:S(2)}) async-start(), calls=%async_computation.1 | async-start | bytes 5308416 | tf_op jit(solution)/shard_map/all_gather | solution.py:71
  8.0 51.7 %copy-start.7 = (f32[768]{0:T(1024)S(1)}, f32[768]{0:T(1024)}, u32[]{:S(2)}) copy-start(f32[768]{0:T(1024)} %param.14) | copy-start | bytes 9220
  8.0 181.8 %all-gather.8.cloned.1.call-start = ((), (), s32[]{:S(2)}) async-start(), calls=%async_computation.2 | async-start | bytes 2654208 | tf_op jit(solution)/shard_map/all_gather | solution.py:78
  59.0 0.8 copy-start.2
  89.4 2.3 %copy-start.1 = (f32[16,64,256]{2,1,0:T(8,128)S(1)}, f32[16,64,256]{2,1,0:T(8,128)}, u32[]{:S(2)}) copy-start(f32[16,64,256]{2,1,0:T(8,128)} %convert_element_type.40) | copy-start | bytes 3145732
  91.6 1.1 copy-start.6
  92.8 1.6 copy-start.5
  93.4 1.3 copy-start.3
  93.4 2.1 %copy-start.8 = (f32[768]{0:T(1024)S(1)}, f32[768]{0:T(1024)}, u32[]{:S(2)}) copy-start(f32[768]{0:T(1024)} %param.17) | copy-start | bytes 9220
  94.7 0.8 copy-start.4
Sparse Core Ops, SparseCore 0:
  9.5 46.8 all-gather.3
  58.6 78.6 all-gather.5
  139.6 50.2 all-gather.7
where the time goes:
time: 204 us
  waiting for transfers between devices  138 us (68%)
  blocking collectives  18.8 us (9%)
  matrix products  15.3 us (8%)
  between operations  13.2 us (6%)
  local copies, waits for them, and re-layouts  10.2 us (5%)
  other arithmetic  8.41 us (4%)
    all_gather x1, waiting for transfers between devices, run_block(): lax.all_gather(w_out, 'particle', axis=0, tiled=True)  49.2 us
    all_gather x1, waiting for transfers between devices, body(): lax.all_gather(states, 'particle', axis=0, tiled=True)  45.5 us
    all_gather x1, waiting for transfers between devices, run_block(): portion = lax.all_gather(w_in, 'particle', axis=1, tiled=True)  40.8 us
    all_gather x1, blocking collectives, run_block(): lax.all_gather(value_local, 'token', axis=1, tiled=True)  9.78 us
    all_gather x1, blocking collectives, run_block(): lax.all_gather(key_local, 'token', axis=1, tiled=True)  9.02 us
    dot_general x1, matrix products, run_block(): jnp.einsum('prf,nf->prn', hidden, lax.all_gather(w_out, 'particle', axis=...  4.77 us
  transfers between devices with their start and end apart: 3, of which 3 were waited for; matrix products, arithmetic and copies ran while one was open for 12% of the time, Pallas kernels for 0%

commit v1 on v0

--- a/solution.py
+++ b/solution.py
@@ -3,7 +3,11 @@
 import jax
 import jax.numpy as jnp
 from jax import lax
+from jax.experimental import pallas as pl
+from jax.experimental.pallas import tpu as pltpu
 from jax.sharding import PartitionSpec as P
+
+MESH = pl.DeviceIdType.MESH
 
 
 def rms_norm(stream, gain_vec):
@@ -49,14 +53,17 @@
         jnp.zeros((part_count, head_count, row_count), jnp.float32),
         jnp.zeros((part_count, head_count, row_count, head_size), jnp.float32),
     )
-    projected = jnp.einsum("prd,de->pre", normed, w_qkv, preferred_element_type=jnp.float32)
-    queries = (projected[..., :model_width] * score_scale).astype(jnp.bfloat16)
-    key_local = projected[..., model_width : 2 * model_width].astype(jnp.bfloat16)
-    value_local = projected[..., 2 * model_width :].astype(jnp.bfloat16)
-    portion = (
-        lax.all_gather(key_local, "token", axis=1, tiled=True),
-        lax.all_gather(value_local, "token", axis=1, tiled=True),
-    )
+    queries = (
+        jnp.einsum(
+            "prd,de->pre", normed, w_qkv[:, :model_width], preferred_element_type=jnp.float32
+        )
+        * score_scale
+    ).astype(jnp.bfloat16)
+    normed_all = lax.all_gather(normed, "token", axis=1, tiled=True)
+    projected = jnp.einsum(
+        "prd,de->pre", normed_all, w_qkv[:, model_width:], preferred_element_type=jnp.float32
+    ).astype(jnp.bfloat16)
+    portion = (projected[..., :model_width], projected[..., model_width:])
     running, totals, summed = attend_portion(
         start_carry, queries, portion[0], portion[1], pair_bias, key_mask
     )
@@ -68,17 +75,15 @@
     )
     stream = stream + jnp.einsum("prd,de->pre", attended, w_o, preferred_element_type=jnp.float32)
     normed_ff = rms_norm(stream, gain_ff).astype(jnp.bfloat16)
-    portion = lax.all_gather(w_in, "particle", axis=1, tiled=True)
-    gate_sum = jnp.einsum("prd,df->prf", normed_ff, portion[0], preferred_element_type=jnp.float32)
-    up_sum = jnp.einsum("prd,df->prf", normed_ff, portion[1], preferred_element_type=jnp.float32)
+    normed_ff = lax.all_gather(normed_ff, "token", axis=1, tiled=True)
+    gate_sum = jnp.einsum("prd,df->prf", normed_ff, w_in[0], preferred_element_type=jnp.float32)
+    up_sum = jnp.einsum("prd,df->prf", normed_ff, w_in[1], preferred_element_type=jnp.float32)
     hidden = (jax.nn.silu(gate_sum) * up_sum).astype(jnp.bfloat16)
     update = jnp.einsum(
-        "prf,nf->prn",
-        hidden,
-        lax.all_gather(w_out, "particle", axis=0, tiled=True),
-        preferred_element_type=jnp.float32,
-    )
-    return (stream + update).astype(jnp.bfloat16)
+        "prf,nf->prn", hidden, w_out, preferred_element_type=jnp.float32
+    ).astype(jnp.bfloat16)
+    update = lax.psum_scatter(update, "token", scatter_dimension=1, tiled=True)
+    return (stream + update.astype(jnp.float32)).astype(jnp.bfloat16)
 
 
 def select_rows(ancestors, portion):
@@ -92,7 +97,400 @@
     chosen = select_rows(ancestors, lax.all_gather(states, "particle", axis=0, tiled=True)).astype(
         jnp.bfloat16
     )
+    units = w_out.shape[1] // lax.axis_size("token")
+    first = lax.axis_index("token") * units
+    w_in = lax.all_gather(
+        lax.dynamic_slice_in_dim(w_in, first, units, 2), "particle", axis=1, tiled=True
+    )
+    w_out = lax.all_gather(
+        lax.dynamic_slice_in_dim(w_out, first, units, 1), "particle", axis=0, tiled=True
+    )
     return run_block(chosen, pair_bias, key_mask, gain_attn, w_qkv, w_o, gain_ff, w_in, w_out)
+
+
+def block_kernel(
+    states_ref, ancestors_ref, bias_hbm, mask_ref, gain_attn_ref, w_qkv_hbm, w_o_hbm, gain_ff_ref,
+    w_in_hbm, w_out_hbm, out_ref,
+    states_all, w_in_all, w_out_all, w_qkv, w_o, bias, normed_all, kv_all, ff_all,
+    core_out, core_in, row_out, row_in,
+    local_sem, recv_sem, right_sem, left_sem, across_sem, gather_recv, gather_row, gather_core,
+    core_send, core_recv, row_send, row_recv,
+):
+    per, rows, width = states_ref.shape
+    groups = lax.axis_size("particle")
+    lines = groups // 2
+    cells = lax.axis_size("token")
+    spans = cells // 2
+    units = w_in_all.shape[-1]
+    head_count = bias.shape[0] // rows
+    head_size = width // head_count
+    me = lax.axis_index("particle")
+    spot = lax.axis_index("token")
+    line, side = me // 2, me % 2
+    span, core = spot // 2, spot % 2
+    across = (line * 2 + 1 - side, spot)
+    above, below = (me + 2, spot), (me - 2, spot)
+    other_core = (me, span * 2 + 1 - core)
+
+    def span_peer(step):
+        return lax.rem(span + step, spans)
+
+    barrier = pltpu.get_barrier_semaphore()
+
+    def greet(device):
+        pl.semaphore_signal(barrier, inc=1, device_id=device, device_id_type=MESH)
+
+    greet(across)
+    greet(other_core)
+    for step in range(1, spans):
+        greet((me, span_peer(step) * 2 + core))
+
+    @pl.when(line > 0)
+    def _():
+        greet(below)
+
+    @pl.when(line < lines - 1)
+    def _():
+        greet(above)
+
+    first = pl.multiple_of(spot * units, 128)
+    locals_ = [
+        pltpu.make_async_copy(states_ref, states_all.at[pl.ds(me * per, per)], local_sem.at[0]),
+        pltpu.make_async_copy(
+            w_in_hbm.at[:, :, pl.ds(first, units)], w_in_all.at[me], local_sem.at[1]
+        ),
+        pltpu.make_async_copy(
+            w_out_hbm.at[:, pl.ds(first, units)], w_out_all.at[me], local_sem.at[2]
+        ),
+        pltpu.make_async_copy(w_qkv_hbm, w_qkv, local_sem.at[3]),
+        pltpu.make_async_copy(bias_hbm, bias, local_sem.at[4]),
+        pltpu.make_async_copy(w_o_hbm, w_o, local_sem.at[5]),
+    ]
+    for copy in locals_:
+        copy.start()
+    locals_[0].wait()
+    pl.semaphore_wait(
+        barrier,
+        2 + spans - 1 + jnp.where(line > 0, 1, 0) + jnp.where(line < lines - 1, 1, 0),
+    )
+
+    views = (
+        lambda k: states_all.at[pl.ds(k * per, per)],
+        lambda k: w_in_all.at[k],
+        lambda k: w_out_all.at[k],
+    )
+
+    def remote(kind, source, sems, device):
+        k = source * 2 + side
+        return pltpu.make_async_remote_copy(
+            src_ref=views[kind](k),
+            dst_ref=views[kind](k),
+            send_sem=sems.at[kind, source],
+            recv_sem=recv_sem.at[kind, k],
+            device_id=device,
+            device_id_type=MESH,
+        )
+
+    def arrived(kind, k):
+        pltpu.make_async_remote_copy(
+            src_ref=views[kind](k),
+            dst_ref=views[kind](k),
+            send_sem=across_sem.at[kind, 0],
+            recv_sem=recv_sem.at[kind, k],
+            device_id=across,
+            device_id_type=MESH,
+        ).wait_recv()
+
+    def relay(kind, step):
+        low, high = line - step, line + step
+
+        @pl.when(low >= 0)
+        def _():
+            if step > 0:
+                arrived(kind, low * 2 + side)
+
+            @pl.when(line < lines - 1)
+            def _():
+                remote(kind, low, right_sem, above).start()
+
+        @pl.when(high < lines)
+        def _():
+            if step > 0:
+                arrived(kind, high * 2 + side)
+
+            @pl.when(line > 0)
+            def _():
+                remote(kind, high, left_sem, below).start()
+
+        @pl.when(low >= 0)
+        def _():
+            remote(kind, low, across_sem, across).start()
+
+        if step > 0:
+
+            @pl.when(high < lines)
+            def _():
+                remote(kind, high, across_sem, across).start()
+
+    def finish(kind):
+        for source in range(lines):
+            arrived(kind, source * 2 + 1 - side)
+
+    def drain(kind):
+        for source in range(lines):
+            remote(kind, source, across_sem, across).wait_send()
+
+            @pl.when(jnp.logical_and(line < lines - 1, source <= line))
+            def _():
+                remote(kind, source, right_sem, above).wait_send()
+
+            @pl.when(jnp.logical_and(line > 0, source >= line))
+            def _():
+                remote(kind, source, left_sem, below).wait_send()
+
+    def slot_copy(which, buf, slot, send, device):
+        return pltpu.make_async_remote_copy(
+            src_ref=buf.at[slot],
+            dst_ref=buf.at[slot],
+            send_sem=send,
+            recv_sem=gather_recv.at[which, slot],
+            device_id=device,
+            device_id_type=MESH,
+        )
+
+    def token_sends(which, buf):
+        copies = [
+            slot_copy(
+                which, buf, spot, gather_row.at[which, step], (me, span_peer(step) * 2 + core)
+            )
+            for step in range(1, spans)
+        ]
+        copies.append(slot_copy(which, buf, spot, gather_core.at[which, 0], other_core))
+        for copy in copies:
+            copy.start()
+        return copies
+
+    def token_forward(which, buf):
+        copies = []
+        for step in range(1, spans):
+            slot = span_peer(step) * 2 + core
+            copy = slot_copy(which, buf, slot, gather_core.at[which, step], other_core)
+            copy.wait_recv()
+            copy.start()
+            copies.append(copy)
+        for step in range(spans):
+            slot = span_peer(step) * 2 + 1 - core
+            slot_copy(which, buf, slot, gather_core.at[which, 0], other_core).wait_recv()
+        return copies
+
+    def norm(stream, gain):
+        mean = jnp.mean(stream * stream, axis=-1, keepdims=True)
+        return (stream * lax.rsqrt(mean + 1e-05) * gain).astype(jnp.bfloat16)
+
+    def dot(a, b):
+        return jnp.dot(a, b, preferred_element_type=jnp.float32)
+
+    def dot_t(a, b):
+        return lax.dot_general(
+            a, b, (((1,), (1,)), ((), ())), preferred_element_type=jnp.float32
+        )
+
+    relay(0, 0)
+    locals_[1].wait()
+    relay(0, 1)
+    relay(1, 0)
+    relay(0, 2) if lines > 2 else None
+    for step in range(3, lines):
+        relay(0, step)
+    locals_[2].wait()
+    relay(2, 0)
+    finish(0)
+
+    stream = jnp.concatenate(
+        [states_all[ancestors_ref[j]].astype(jnp.float32) for j in range(per)], axis=0
+    )
+    normed = norm(stream, gain_attn_ref[...])
+    normed_all[spot] = normed
+    sent = token_sends(0, normed_all)
+    if lines > 1:
+        relay(1, 1)
+    locals_[3].wait()
+    scale = 1.0 / math.sqrt(head_size)
+    queries = (dot(normed, w_qkv[:, :width]) * scale).astype(jnp.bfloat16)
+    sent += token_forward(0, normed_all)
+    if lines > 1:
+        relay(2, 1)
+    kv_all[...] = dot(
+        normed_all[...].reshape(cells * per * rows, width), w_qkv[:, width:]
+    ).astype(jnp.bfloat16)
+    if lines > 2:
+        relay(1, 2)
+    locals_[4].wait()
+    usable = mask_ref[...] > 0
+    half = 8
+    strip = half * head_size
+    lane = lax.broadcasted_iota(jnp.int32, (half, 1, strip), 2)
+    head = lax.broadcasted_iota(jnp.int32, (half, 1, strip), 0)
+    mine = jnp.logical_and(lane >= head * head_size, lane < (head + 1) * head_size)
+    mine_bf = mine.astype(jnp.float32).astype(jnp.bfloat16)
+    mine_f = mine.astype(jnp.float32)
+    mixed = []
+    for j in range(per):
+        strips = []
+        for part in range(head_count // half):
+            cols = slice(part * strip, (part + 1) * strip)
+            q = queries[j * rows : (j + 1) * rows, cols]
+            spread = (q[None] * mine_bf).reshape(half * rows, strip)
+
+            def tokens_of(base):
+                return jnp.concatenate(
+                    [
+                        kv_all[
+                            (t * per + j) * rows : (t * per + j + 1) * rows,
+                            base + part * strip : base + (part + 1) * strip,
+                        ]
+                        for t in range(cells)
+                    ],
+                    axis=0,
+                )
+
+            scores = dot_t(spread, tokens_of(0)) + bias[
+                part * half * rows : (part + 1) * half * rows, :
+            ].astype(jnp.float32)
+            scores = jnp.where(usable, scores, -1e30)
+            top = jnp.max(scores, axis=1, keepdims=True)
+            weights = jnp.where(usable, jnp.exp(scores - top), 0.0)
+            total = jnp.sum(weights, axis=1, keepdims=True)
+            mix = dot(weights.astype(jnp.bfloat16), tokens_of(width)) / total
+            strips.append(jnp.sum(mix.reshape(half, rows, strip) * mine_f, axis=0))
+        mixed.append(jnp.concatenate(strips, axis=1))
+    attended = jnp.concatenate(mixed, axis=0).astype(jnp.bfloat16)
+    if lines > 2:
+        relay(2, 2)
+    locals_[5].wait()
+    stream = stream + dot(attended, w_o[...])
+    ff_all[spot] = norm(stream, gain_ff_ref[...])
+    sent += token_sends(1, ff_all)
+    for step in range(3, lines):
+        relay(1, step)
+        relay(2, step)
+    sent += token_forward(1, ff_all)
+    finish(1)
+    normed_ff = ff_all[...].reshape(cells * per * rows, width)
+    gate = dot(normed_ff, w_in_all[:, 0].reshape(width, units))
+    up = dot(normed_ff, w_in_all[:, 1].reshape(width, units))
+    hidden = (gate / (1.0 + jnp.exp(-gate)) * up).astype(jnp.bfloat16)
+    finish(2)
+    update = dot_t(hidden, w_out_all[...].reshape(width, units))
+    update = update.reshape(spans, 2, per * rows, width)
+    is_low = core == 0
+    core_out[...] = jnp.where(is_low, update[:, 1], update[:, 0]).astype(jnp.bfloat16)
+    copy = pltpu.make_async_remote_copy(
+        src_ref=core_out,
+        dst_ref=core_in,
+        send_sem=core_send,
+        recv_sem=core_recv,
+        device_id=other_core,
+        device_id_type=MESH,
+    )
+    copy.start()
+    kept = jnp.where(is_low, update[:, 0], update[:, 1])
+    copy.wait_recv()
+    sent.append(copy)
+    row_out[...] = (kept + core_in[...].astype(jnp.float32)).astype(jnp.bfloat16)
+    rowed = []
+    for step in range(1, spans):
+        copy = pltpu.make_async_remote_copy(
+            src_ref=row_out.at[span_peer(step)],
+            dst_ref=row_in.at[step],
+            send_sem=row_send.at[step],
+            recv_sem=row_recv.at[step],
+            device_id=(me, span_peer(step) * 2 + core),
+            device_id_type=MESH,
+        )
+        copy.start()
+        rowed.append(copy)
+    stream = stream + row_out[span].astype(jnp.float32)
+    for step, copy in enumerate(rowed, 1):
+        copy.wait_recv()
+        stream = stream + row_in[step].astype(jnp.float32)
+    out_ref[...] = stream.astype(jnp.bfloat16).reshape(per, rows, width)
+    for copy in sent + rowed:
+        copy.wait_send()
+    for kind in range(3):
+        drain(kind)
+
+
+def fused_body(
+    states, ancestors, pair_bias, key_mask, gain_attn, w_qkv, w_o, gain_ff, w_in, w_out
+):
+    per, rows, width = states.shape
+    groups, cells = lax.axis_size("particle"), lax.axis_size("token")
+    lines, spans = groups // 2, cells // 2
+    units = w_out.shape[1] // cells
+    depth = w_in.shape[1]
+    heads, _, keys = pair_bias.shape
+    vmem = pl.BlockSpec(memory_space=pltpu.VMEM)
+    smem = pl.BlockSpec(memory_space=pltpu.SMEM)
+    hbm = pl.BlockSpec(memory_space=pl.ANY)
+    dma = pltpu.SemaphoreType.DMA
+    bf16 = jnp.bfloat16
+    block = (per * rows, width)
+    return pl.pallas_call(
+        block_kernel,
+        out_shape=jax.ShapeDtypeStruct(states.shape, bf16),
+        in_specs=[vmem, smem, hbm, vmem, vmem, hbm, hbm, vmem, hbm, hbm],
+        out_specs=vmem,
+        scratch_shapes=[
+            pltpu.VMEM((groups * per, rows, width), bf16),
+            pltpu.VMEM((groups, 2, depth, units), bf16),
+            pltpu.VMEM((groups, depth, units), bf16),
+            pltpu.VMEM(w_qkv.shape, bf16),
+            pltpu.VMEM(w_o.shape, bf16),
+            pltpu.VMEM((heads * rows, keys), bf16),
+            pltpu.VMEM((cells,) + block, bf16),
+            pltpu.VMEM((cells * per * rows, 2 * width), bf16),
+            pltpu.VMEM((cells,) + block, bf16),
+            pltpu.VMEM((spans,) + block, bf16),
+            pltpu.VMEM((spans,) + block, bf16),
+            pltpu.VMEM((spans,) + block, bf16),
+            pltpu.VMEM((spans,) + block, bf16),
+            dma((6,)),
+            dma((3, groups)),
+            dma((3, lines)),
+            dma((3, lines)),
+            dma((3, lines)),
+            dma((2, cells)),
+            dma((2, spans)),
+            dma((2, spans)),
+            dma,
+            dma,
+            dma((spans,)),
+            dma((spans,)),
+        ],
+        compiler_params=pltpu.CompilerParams(
+            collective_id=0, has_side_effects=True, vmem_limit_bytes=56 * 1024 * 1024
+        ),
+    )(
+        states,
+        ancestors,
+        pair_bias.reshape(heads * rows, keys),
+        key_mask.reshape(1, keys),
+        gain_attn.reshape(1, width),
+        w_qkv,
+        w_o,
+        gain_ff.reshape(1, width),
+        w_in,
+        w_out,
+    )
+
+
+def either_body(states, ancestors, pair_bias, key_mask, gain_attn, w_qkv, w_o, gain_ff, w_in, w_out):
+    tiles = w_in.shape[1] % 16 == 0 and (w_out.shape[1] // lax.axis_size("token")) % 128 == 0
+    run = fused_body if tiles else body
+    return run(
+        states, ancestors, pair_bias, key_mask, gain_attn, w_qkv, w_o, gain_ff, w_in, w_out
+    )
 
 
 def solution(mesh):
@@ -109,5 +507,5 @@
         P("particle", None),
     )
     return jax.shard_map(
-        body, mesh=mesh, in_specs=placed, out_specs=P("particle", "token", None), check_vma=False
-    )
+        either_body, mesh=mesh, in_specs=placed, out_specs=P("particle", "token", None), check_vma=False
+    )

time: 204 us -> 62.9 us (0.31)
  waiting for transfers between devices: 138 us -> 0 us
  Pallas kernels: 0 us -> 58.5 us
  blocking collectives: 18.8 us -> 0 us
  matrix products: 15.3 us -> 0 us
  between operations: 13.2 us -> 0.01 us
  other arithmetic: 8.41 us -> 0 us
  local copies, waits for them, and re-layouts: 10.2 us -> 4.15 us
    all_gather x3 -> x0, waiting for transfers between devices: 136 us -> none  [the longest x1 49.2 us: run_block(): lax.all_gather(w_out, 'particle', axis=0, tiled=True)]
    pallas_call x0 -> x1, Pallas kernels: none -> 58.5 us  [fused_body(): pl.pallas_call(block_kernel, out_shape=jax.ShapeDtypeStruct(states.shape,...]
    all_gather x2 -> x0, blocking collectives: 18.8 us -> none  [the longest x1 9.78 us: run_block(): lax.all_gather(value_local, 'token', axis=1, tiled=True)]
    dot_general x7 -> x0, matrix products: 15.3 us -> none  [the longest x1 4.77 us: run_block(): jnp.einsum('prf,nf->prn', hidden, lax.all_gather(w_out, 'particle', axis=...]
    convert_element_type x5 -> x0, other arithmetic: 7.1 us -> none  [the longest x1 2.19 us: attend_portion(): bias_part = pair_bias.astype(jnp.float32)]
    all_gather x2 -> x0, local copies, waits for them, and re-layouts: 4.66 us -> none  [the longest x1 2.37 us: run_block(): lax.all_gather(key_local, 'token', axis=1, tiled=True)]
    unnamed x3 -> x0, waiting for transfers between devices: 2.08 us -> none
  transfers between devices with their start and end apart: 3 -> 0, of which waited for: 3 -> 0; matrix products, arithmetic and copies ran while one was open for 12% -> 0% of each run, Pallas kernels for 0% -> 0%
where the time goes in v1:
time: 62.9 us; the launch traced here: 62.7 us
  Pallas kernels  58.5 us (93%)
  local copies, waits for them, and re-layouts  4.15 us (7%)
    pallas_call x1, Pallas kernels, fused_body(): pl.pallas_call(block_kernel, out_shape=jax.ShapeDtypeStruct(states.shape,...  58.5 us
    unnamed x1, local copies, waits for them, and re-layouts  1.62 us
    reshape x1, local copies, waits for them, and re-layouts, fused_body(): gain_attn.reshape(1, width)  1.27 us
    reshape x1, local copies, waits for them, and re-layouts, fused_body(): gain_ff.reshape(1, width)  1.27 us

profile of v1, /device:TPU:0, one launch (start us, length us, event | category | flops | bytes accessed | tf_op | source)
XLA Modules:
  0.0 62.7 jit_solution(8667005485206400656)
XLA Ops:
  0.0 1.3 %reshape.14.gain_attn_ref = f32[1,768]{1,0:T(1,128)} reshape(f32[768]{0:T(1024)} %param.14) | data formatting | bytes 6144 | tf_op jit(solution)/shard_map/reshape | solution.py:479
  1.3 1.3 %reshape.15.gain_ff_ref = f32[1,768]{1,0:T(1,128)} reshape(f32[768]{0:T(1024)} %param.17) | data formatting | bytes 6144 | tf_op jit(solution)/shard_map/reshape | solution.py:482
  2.5 58.5 %shard_map.100 = bf16[2,64,768]{2,1,0:T(8,128)(2,1)} custom-call(bf16[2,64,768]{2,1,0:T(8,128)(2,1)} %states_ref.1, s32[2]{0:T(128)} %ancestors_ref.1, bf16[1024,256]{1,0:T(8,128)(2,1)} %bitcast.2, s32[1,256]{1,0:T(1,128)} %bitcast.3, f32[1,768]{1,0:T(1,128)} %reshape.14.gain_attn_ref, bf16[768,2304]{1,0:T(8,128)(2,1)} %w_qkv_hbm.1, ...), custom_call_target="tpu_custom_call" | custom-call | tf_op jit(solution)/shard_map/pallas_call | solution.py:439
  61.0 1.6 %copy.12 = bf16[2,64,768]{2,1,0:T(8,128)(2,1)} copy(bf16[2,64,768]{2,1,0:T(8,128)(2,1)} %shard_map.100) | data formatting | bytes 393216

commit v2 on v1

--- a/solution.py
+++ b/solution.py
@@ -112,9 +112,9 @@
     states_ref, ancestors_ref, bias_hbm, mask_ref, gain_attn_ref, w_qkv_hbm, w_o_hbm, gain_ff_ref,
     w_in_hbm, w_out_hbm, out_ref,
     states_all, w_in_all, w_out_all, w_qkv, w_o, bias, normed_all, kv_all, ff_all,
-    core_out, core_in, row_out, row_in,
+    core_out, core_in, row_out, row_in, wish_out, wish_in, pick_out, pick_in,
     local_sem, recv_sem, right_sem, left_sem, across_sem, gather_recv, gather_row, gather_core,
-    core_send, core_recv, row_send, row_recv,
+    core_send, core_recv, row_send, row_recv, wish_send, wish_recv, pick_send, pick_recv,
 ):
     per, rows, width = states_ref.shape
     groups = lax.axis_size("particle")
@@ -201,7 +201,7 @@
             device_id_type=MESH,
         ).wait_recv()
 
-    def relay(kind, step):
+    def relay(kind, step, along=True, cross=True):
         low, high = line - step, line + step
 
         @pl.when(low >= 0)
@@ -209,7 +209,7 @@
             if step > 0:
                 arrived(kind, low * 2 + side)
 
-            @pl.when(line < lines - 1)
+            @pl.when(jnp.logical_and(along, line < lines - 1))
             def _():
                 remote(kind, low, right_sem, above).start()
 
@@ -218,9 +218,12 @@
             if step > 0:
                 arrived(kind, high * 2 + side)
 
-            @pl.when(line > 0)
+            @pl.when(jnp.logical_and(along, line > 0))
             def _():
                 remote(kind, high, left_sem, below).start()
+
+        if kind == 0 or not cross:
+            return
 
         @pl.when(low >= 0)
         def _():
@@ -238,7 +241,8 @@
 
     def drain(kind):
         for source in range(lines):
-            remote(kind, source, across_sem, across).wait_send()
+            if kind > 0:
+                remote(kind, source, across_sem, across).wait_send()
 
             @pl.when(jnp.logical_and(line < lines - 1, source <= line))
             def _():
@@ -295,38 +299,69 @@
             a, b, (((1,), (1,)), ((), ())), preferred_element_type=jnp.float32
         )
 
+    for j in range(per):
+        wish_out[j] = jnp.full(wish_out.shape[1:], ancestors_ref[j], jnp.int32)
+
+    def to_across(source, target, send, recv):
+        return pltpu.make_async_remote_copy(
+            src_ref=source,
+            dst_ref=target,
+            send_sem=send,
+            recv_sem=recv,
+            device_id=across,
+            device_id_type=MESH,
+        )
+
+    wish = to_across(wish_out, wish_in, wish_send, wish_recv)
+    wish.start()
     relay(0, 0)
     locals_[1].wait()
-    relay(0, 1)
-    relay(1, 0)
-    relay(0, 2) if lines > 2 else None
-    for step in range(3, lines):
+    relay(1, 0, along=False)
+    locals_[2].wait()
+    relay(2, 0, along=False)
+    for step in range(1, lines - 1):
         relay(0, step)
-    locals_[2].wait()
-    relay(2, 0)
-    finish(0)
-
+    relay(1, 0, cross=False)
+    if lines > 1:
+        relay(0, lines - 1)
+    wish.wait_recv()
+
+    def picked(wishes):
+        found = [jnp.zeros((rows, width), jnp.float32) for _ in range(per)]
+        for source in range(lines):
+            for i in range(per):
+                k = (source * 2 + side) * per + i
+                held = states_all[k].astype(jnp.float32)
+                for j in range(per):
+                    found[j] = jnp.where(wishes[j][:1, :1] == k, held, found[j])
+        return found
+
+    for j, found in enumerate(picked([wish_in[j] for j in range(per)])):
+        pick_out[j] = found.astype(jnp.bfloat16)
+    pick = to_across(pick_out, pick_in, pick_send, pick_recv)
+    pick.start()
+    own = picked([wish_out[j] for j in range(per)])
+    pick.wait_recv()
     stream = jnp.concatenate(
-        [states_all[ancestors_ref[j]].astype(jnp.float32) for j in range(per)], axis=0
-    )
-    normed = norm(stream, gain_attn_ref[...])
+        [own[j] + pick_in[j].astype(jnp.float32) for j in range(per)], axis=0
+    )
+    normed = norm(stream, gain_attn_ref[...].reshape(1, width))
     normed_all[spot] = normed
     sent = token_sends(0, normed_all)
-    if lines > 1:
-        relay(1, 1)
     locals_[3].wait()
     scale = 1.0 / math.sqrt(head_size)
     queries = (dot(normed, w_qkv[:, :width]) * scale).astype(jnp.bfloat16)
     sent += token_forward(0, normed_all)
     if lines > 1:
-        relay(2, 1)
+        relay(1, 1)
     kv_all[...] = dot(
         normed_all[...].reshape(cells * per * rows, width), w_qkv[:, width:]
     ).astype(jnp.bfloat16)
-    if lines > 2:
-        relay(1, 2)
+    for step in range(2, lines - 1):
+        relay(1, step)
+    relay(2, 0, cross=False)
     locals_[4].wait()
-    usable = mask_ref[...] > 0
+    usable = mask_ref[...].reshape(1, -1) > 0
     half = 8
     strip = half * head_size
     lane = lax.broadcasted_iota(jnp.int32, (half, 1, strip), 2)
@@ -364,16 +399,19 @@
             mix = dot(weights.astype(jnp.bfloat16), tokens_of(width)) / total
             strips.append(jnp.sum(mix.reshape(half, rows, strip) * mine_f, axis=0))
         mixed.append(jnp.concatenate(strips, axis=1))
+        if j == 0 and lines > 1:
+            if lines > 2:
+                relay(1, lines - 1)
+            relay(2, 1)
     attended = jnp.concatenate(mixed, axis=0).astype(jnp.bfloat16)
-    if lines > 2:
-        relay(2, 2)
+    for step in range(2, lines - 1):
+        relay(2, step)
     locals_[5].wait()
     stream = stream + dot(attended, w_o[...])
-    ff_all[spot] = norm(stream, gain_ff_ref[...])
+    ff_all[spot] = norm(stream, gain_ff_ref[...].reshape(1, width))
     sent += token_sends(1, ff_all)
-    for step in range(3, lines):
-        relay(1, step)
-        relay(2, step)
+    if lines > 2:
+        relay(2, lines - 1)
     sent += token_forward(1, ff_all)
     finish(1)
     normed_ff = ff_all[...].reshape(cells * per * rows, width)
@@ -415,7 +453,7 @@
         copy.wait_recv()
         stream = stream + row_in[step].astype(jnp.float32)
     out_ref[...] = stream.astype(jnp.bfloat16).reshape(per, rows, width)
-    for copy in sent + rowed:
+    for copy in sent + rowed + [wish, pick]:
         copy.wait_send()
     for kind in range(3):
         drain(kind)
@@ -455,6 +493,10 @@
             pltpu.VMEM((spans,) + block, bf16),
             pltpu.VMEM((spans,) + block, bf16),
             pltpu.VMEM((spans,) + block, bf16),
+            pltpu.VMEM((per, 8, 128), jnp.int32),
+            pltpu.VMEM((per, 8, 128), jnp.int32),
+            pltpu.VMEM((per, rows, width), bf16),
+            pltpu.VMEM((per, rows, width), bf16),
             dma((6,)),
             dma((3, groups)),
             dma((3, lines)),
@@ -467,6 +509,10 @@
             dma,
             dma((spans,)),
             dma((spans,)),
+            dma,
+            dma,
+            dma,
+            dma,
         ],
         compiler_params=pltpu.CompilerParams(
             collective_id=0, has_side_effects=True, vmem_limit_bytes=56 * 1024 * 1024
@@ -475,11 +521,11 @@
         states,
         ancestors,
         pair_bias.reshape(heads * rows, keys),
-        key_mask.reshape(1, keys),
-        gain_attn.reshape(1, width),
+        key_mask,
+        gain_attn,
         w_qkv,
         w_o,
-        gain_ff.reshape(1, width),
+        gain_ff,
         w_in,
         w_out,
     )

time: 62.9 us -> 62.9 us (level)
  Pallas kernels: 58.5 us -> 61.2 us
  local copies, waits for them, and re-layouts: 4.15 us -> 1.62 us
    pallas_call x1, Pallas kernels: 58.5 us -> 61.2 us  [fused_body(): pl.pallas_call(block_kernel, out_shape=jax.ShapeDtypeStruct(states.shape,...]
    reshape x2 -> x0, local copies, waits for them, and re-layouts: 2.53 us -> none  [the longest x1 1.27 us: fused_body(): gain_attn.reshape(1, width)]
where the time goes in v2:
time: 62.9 us; the launch traced here: 62.8 us
  Pallas kernels  61.2 us (97%)
  local copies, waits for them, and re-layouts  1.62 us (3%)
    pallas_call x1, Pallas kernels, fused_body(): pl.pallas_call(block_kernel, out_shape=jax.ShapeDtypeStruct(states.shape,...  61.2 us
    unnamed x1, local copies, waits for them, and re-layouts  1.62 us

profile of v2, /device:TPU:0, one launch (start us, length us, event | category | flops | bytes accessed | tf_op | source)
XLA Modules:
  0.0 62.8 jit_solution(17909645499908677250)
XLA Ops:
  0.0 61.2 %shard_map.100 = bf16[2,64,768]{2,1,0:T(8,128)(2,1)} custom-call(bf16[2,64,768]{2,1,0:T(8,128)(2,1)} %states_ref.1, s32[2]{0:T(128)} %ancestors_ref.1, bf16[1024,256]{1,0:T(8,128)(2,1)} %bitcast.1, s32[256]{0:T(256)} %mask_ref.1, f32[768]{0:T(1024)} %gain_attn_ref.1, bf16[768,2304]{1,0:T(8,128)(2,1)} %w_qkv_hbm.1, bf16[768,768]{1,0:T(8,128)(2,1)} %w_o_hbm.1, ...), custom_call_target="tpu_custom_call" | custom-call | tf_op jit(solution)/shard_map/pallas_call | solution.py:477
  61.2 1.6 %copy.12 = bf16[2,64,768]{2,1,0:T(8,128)(2,1)} copy(bf16[2,64,768]{2,1,0:T(8,128)(2,1)} %shard_map.100) | data formatting | bytes 393216
